TPU v7x, 32 devices: a whole 2x2x4 slice. The times are simulated.
32 devices in a mesh: groups: 2 (over y), adapter: 4 (over z), head: 4 (over x, core).
Axes of the slice: x: 2, y: 2, z: 4, core: 2. Of those that a mesh axis runs over, the one named last changes fastest.
Arguments:
- normed_hidden_rows: bfloat16 [256, 8192], P(('groups', 'adapter'), 'head'), parts along dimension 0, may hold values from -6 to 6
- base_query: bfloat16 [256, 8192], P(('groups', 'adapter'), 'head'), parts along dimension 0, may hold values from -6 to 6
- base_key_value: bfloat16 [256, 2, 1024], P(('groups', 'adapter'), None, 'head'), parts along dimension 0, may hold values from -6 to 6
- key_value_cache: bfloat16 [2560, 2, 16, 1024], P(('groups', 'adapter'), None, None, 'head'), parts along dimension 0, may hold values from -6 to 6
- cached_length_per_request: int32 [256], P(('groups', 'adapter')), parts along dimension 0, may hold values from 1 to 2560, as said below
- request_page_table: int32 [256, 160], P(('groups', 'adapter')), parts along dimension 0, may hold values from 0 to 319, as said below
- planned_request_rows: int32 [256], P('groups'), parts along dimension 0, may hold values from 0 to 127, as said below
- request_adapters: int32 [256], P('groups'), parts along dimension 0, may hold values from 0 to 15, as said below
- query_key_value_down_maps: bfloat16 [16, 8192, 96], P('adapter', 'head'), may hold values from -0.0625 to 0.0625
- query_up_maps: bfloat16 [16, 32, 8192], P('adapter', None, 'head'), may hold values from -1 to 1
- key_value_up_maps: bfloat16 [16, 2, 32, 1024], P('adapter', None, None, 'head'), may hold values from -1 to 1
- output_down_maps: bfloat16 [16, 8192, 32], P('adapter', 'head'), may hold values from -0.25 to 0.25
- output_up_maps: bfloat16 [16, 32, 8192], P('adapter', 'head'), may hold values from -1 to 1
- output_weight_matrix: bfloat16 [8192, 8192], P('head', 'adapter'), may hold values from -0.25 to 0.25
Outputs:
- block_out: bfloat16 [256, 8192], P(('groups', 'head'), 'adapter'), parts along dimension 0
There are 2 independent parts, one for each index of `groups`. A program takes and returns all parts, laid end to end along the dimension named above; an argument that names none is the same for every part. Nothing has to cross between parts.
Inputs may be any that keep to these rules, and one draw needn't show every extreme that they name: `planned_request_rows`: A permutation. Planned rows k * 32 to (k + 1) * 32 - 1 are the requests of home k. `request_adapters`: adapter i is owned by index i // 4 of adapter. Among the 32 planned rows of one home, at most 16 use adapters of any one owner; in every draw one owner takes exactly 16 rows from every home. `cached_length_per_request`: on each home the requests need ceil(length / 16) pages each and at most 320 in all; one request of each home holds exactly 2560 tokens. `request_page_table`: entries index the pool of the request's home. The 160 entries of a row are distinct; the first ceil(length / 16) of them are pages of that request alone, the rest are other pages of the same pool.
All inputs are finite; a program needn't handle non-finite values.
Results may differ from a plain program's by a relative error of at most 0.0075.
Values may be sent and summed in bfloat16 or wider, within the bound.
A program may use at most 128 MiB of HBM per device.

v0:
```python
import jax
import jax.numpy as jnp
from jax import lax
from jax.sharding import PartitionSpec as P

QH = 64
KVH = 8
HD = 128


def body(
    normed_hidden_rows,
    base_query,
    base_key_value,
    key_value_cache,
    cached_length_per_request,
    request_page_table,
    planned_request_rows,
    request_adapters,
    query_key_value_down_maps,
    query_up_maps,
    key_value_up_maps,
    output_down_maps,
    output_up_maps,
    output_weight_matrix,
):
    home_count = lax.axis_size("adapter")
    my_home = lax.axis_index("adapter")
    req_rows = normed_hidden_rows.shape[0]
    row_total = planned_request_rows.shape[0]
    adapter_in_home = query_key_value_down_maps.shape[0]
    adapter_rank_width = output_down_maps.shape[2]
    slot_count = max(2, 2 * req_rows // home_count)
    spread = home_count * slot_count
    q_width = base_query.shape[1]
    kv_width = base_key_value.shape[2]
    kv_local = kv_width // HD
    group_size = QH // KVH
    zero_value = jnp.zeros((), jnp.bfloat16)
    everyone = jnp.arange(row_total, dtype=jnp.int32)
    matches = planned_request_rows[:, None] == everyone[None, :]
    row_ids = jnp.sum(jnp.where(matches, request_adapters[None, :], 0), axis=1)
    owners = row_ids // adapter_in_home
    within = row_ids % adapter_in_home
    owner_grid = owners.reshape(home_count, req_rows)
    row_order = jnp.arange(req_rows, dtype=jnp.int32)
    before = (owner_grid[:, :, None] == owner_grid[:, None, :]) & (
        row_order[None, None, :] < row_order[None, :, None]
    )
    slot_of = jnp.sum(before, axis=2).reshape(row_total)
    position = everyone // req_rows * slot_count + slot_of
    targets = owners * slot_count + slot_of
    buffer_cells = jnp.arange(spread, dtype=jnp.int32)
    owned_cell = (owners[None, :] == my_home) & (position[None, :] == buffer_cells[:, None])
    source_row = jnp.sum(jnp.where(owned_cell, everyone[None, :], 0), axis=1)
    filled = jnp.any(owned_cell, axis=1)
    source_local = jnp.sum(jnp.where(owned_cell, within[None, :], 0), axis=1)
    adapter_slots = jnp.arange(adapter_in_home, dtype=jnp.int32)
    chooser = ((source_local[:, None] == adapter_slots[None, :]) & filled[:, None]).astype(
        jnp.bfloat16
    )
    chooser_wide = chooser.astype(jnp.float32)
    my_targets = lax.dynamic_slice_in_dim(targets, my_home * req_rows, req_rows)
    sent_cell = my_targets[None, :] == buffer_cells[:, None]
    row_of = jnp.sum(jnp.where(sent_cell, row_order[None, :], 0), axis=1)
    sent_used = jnp.any(sent_cell, axis=1)
    outgoing = jnp.where(
        sent_used[:, None], jnp.take(normed_hidden_rows, row_of, axis=0), zero_value
    )
    received_rows = lax.all_to_all(
        outgoing.reshape(home_count, slot_count, -1),
        "adapter",
        split_axis=0,
        concat_axis=0,
        tiled=True,
    ).reshape(spread, -1)
    partial_value = jnp.einsum(
        "oa,qas->oqs", received_rows, query_key_value_down_maps, preferred_element_type=jnp.float32
    )
    partial_value = jnp.sum(partial_value * chooser_wide[:, :, None], axis=1)
    rank_values = lax.psum(partial_value, "head").astype(jnp.bfloat16)
    selected_maps = chooser[:, :, None] * rank_values[:, None, :]
    delta_q = jnp.einsum(
        "yiw,iwk->yk",
        selected_maps[:, :, :adapter_rank_width],
        query_up_maps,
        preferred_element_type=jnp.float32,
    )
    delta_k = jnp.einsum(
        "yiw,iwk->yk",
        selected_maps[:, :, adapter_rank_width : 2 * adapter_rank_width],
        key_value_up_maps[:, 0],
        preferred_element_type=jnp.float32,
    )
    delta_v = jnp.einsum(
        "yiw,iwk->yk",
        selected_maps[:, :, 2 * adapter_rank_width :],
        key_value_up_maps[:, 1],
        preferred_element_type=jnp.float32,
    )
    deltas = (0.5 * jnp.concatenate([delta_q, delta_k, delta_v], axis=1)).astype(jnp.bfloat16)
    returned = lax.all_to_all(
        deltas.reshape(home_count, slot_count, -1),
        "adapter",
        split_axis=0,
        concat_axis=0,
        tiled=True,
    ).reshape(spread, -1)
    mine_rows = jnp.take(returned, my_targets, axis=0).astype(jnp.float32)
    query_rows = (base_query.astype(jnp.float32) + mine_rows[:, :q_width]).astype(jnp.bfloat16)
    key_new = (
        base_key_value[:, 0].astype(jnp.float32) + mine_rows[:, q_width : q_width + kv_width]
    ).astype(jnp.bfloat16)
    value_new = (
        base_key_value[:, 1].astype(jnp.float32) + mine_rows[:, q_width + kv_width :]
    ).astype(jnp.bfloat16)
    pool_pages = key_value_cache.shape[0]
    page_len = key_value_cache.shape[2]
    same_page = (
        request_page_table[:, :, None] == jnp.arange(pool_pages, dtype=jnp.int32)[None, None, :]
    )
    entry_index = jnp.arange(request_page_table.shape[1], dtype=jnp.int32)
    page_index = jnp.sum(jnp.where(same_page, entry_index[None, :, None], 0), axis=1)
    present = jnp.any(same_page, axis=1)
    token_pos = (
        page_index[:, :, None] * page_len + jnp.arange(page_len, dtype=jnp.int32)[None, None, :]
    )
    visible = (
        present[:, :, None] & (token_pos < cached_length_per_request[:, None, None])
    ).reshape(req_rows, pool_pages * page_len)
    pool_keys = key_value_cache[:, 0].reshape(pool_pages * page_len, kv_local, HD)
    pool_values = key_value_cache[:, 1].reshape(pool_pages * page_len, kv_local, HD)
    queries = query_rows.reshape(req_rows, kv_local, group_size, HD)
    score_scale = HD ** (-0.5)
    scores = (
        jnp.einsum("ikgd,tkd->ikgt", queries, pool_keys, preferred_element_type=jnp.float32)
        * score_scale
    )
    own_score = (
        jnp.einsum(
            "ikgd,ikd->ikg",
            queries,
            key_new.reshape(req_rows, kv_local, HD),
            preferred_element_type=jnp.float32,
        )
        * score_scale
    )
    scores = jnp.where(visible[:, None, None, :], scores, -jnp.inf)
    row_top = jnp.maximum(jnp.max(scores, axis=3), own_score)
    weights = jnp.exp(scores - row_top[..., None])
    own_weight = jnp.exp(own_score - row_top)
    weight_sum = jnp.sum(weights, axis=3) + own_weight
    probabilities = (weights / weight_sum[..., None]).astype(jnp.bfloat16)
    own_probability = (own_weight / weight_sum).astype(jnp.bfloat16)
    mixed_heads = jnp.einsum(
        "ikgt,tkd->ikgd", probabilities, pool_values, preferred_element_type=jnp.float32
    )
    mixed_heads = mixed_heads + own_probability.astype(jnp.float32)[..., None] * value_new.reshape(
        req_rows, kv_local, 1, HD
    ).astype(jnp.float32)
    attended = mixed_heads.reshape(req_rows, q_width).astype(jnp.bfloat16)
    every_attended = lax.all_gather(attended, "adapter", axis=0, tiled=True)
    partials = jnp.dot(every_attended, output_weight_matrix, preferred_element_type=jnp.float32)
    attention_slot_rows = jnp.where(
        filled[:, None], jnp.take(every_attended, source_row, axis=0), zero_value
    )
    output_piece = jnp.einsum(
        "oa,qas->oqs", attention_slot_rows, output_down_maps, preferred_element_type=jnp.float32
    )
    output_piece = jnp.sum(output_piece * chooser_wide[:, :, None], axis=1)
    column_width = output_weight_matrix.shape[1]
    rank_block = lax.psum_scatter(output_piece, "head", scatter_dimension=1, tiled=True).astype(
        jnp.bfloat16
    )
    output_selected = chooser[:, :, None] * rank_block[:, None, :]
    expanded_rows = 0.5 * jnp.einsum(
        "frx,rxv->fv", output_selected, output_up_maps, preferred_element_type=jnp.float32
    )
    landed = lax.all_to_all(
        expanded_rows.reshape(spread, home_count, column_width),
        "adapter",
        split_axis=1,
        concat_axis=0,
        tiled=True,
    ).reshape(home_count * spread, column_width)
    row_delta = jnp.take(landed, owners * spread + position, axis=0)
    terms = partials + row_delta
    base_rows = lax.psum_scatter(terms, "head", scatter_dimension=0, tiled=True)
    return base_rows.astype(jnp.bfloat16)


def solution(mesh):
    return jax.shard_map(
        body,
        mesh=mesh,
        in_specs=(
            P(("groups", "adapter"), "head"),
            P(("groups", "adapter"), "head"),
            P(("groups", "adapter"), None, "head"),
            P(("groups", "adapter"), None, None, "head"),
            P(("groups", "adapter")),
            P(("groups", "adapter"), None),
            P("groups"),
            P("groups"),
            P("adapter", "head", None),
            P("adapter", None, "head"),
            P("adapter", None, None, "head"),
            P("adapter", "head", None),
            P("adapter", "head", None),
            P("head", "adapter"),
        ),
        out_specs=P(("groups", "head"), "adapter"),
        check_vma=False,
    )
```

profile of v0, /device:TPU:0, one launch (start us, length us, event | category | flops | bytes accessed | tf_op | source)
XLA Modules:
  0.0 196.1 jit_solution(812639531303622846)
XLA Ops:
  6.5 1.0 select_reduce_fusion.1
  8.4 1.9 gather_fusion
  10.3 0.8 select_select_fusion
  11.1 6.3 %all-to-all-start = ((bf16[4,16,2048]{2,1,0:T(8,128)(2,1)}), bf16[4,16,2048]{2,1,0:T(8,128)(2,1)S(1)}, u32[]{:S(2)}, u32[]{:S(2)}) async-start(bf16[4,16,2048]{2,1,0:T(8,128)(2,1)} %select_select_fusion), calls=%async_computation | async-start | bytes 524288 | tf_op jit(solution)/shard_map/all_to_all | solution.py:70
  17.5 2.4 %fusion.3 = pred[32,320]{1,0:T(8,128)(4,1)S(1)} fusion(s32[32,160]{1,0:T(8,128)} %param.19), kind=kLoop, calls=%fused_computation.14 | loop fusion | flops 3266560 | bytes 30720 | tf_op jit(solution)/shard_map/reduce_or | solution.py:124
  19.9 2.4 %select_reduce_fusion = s32[32,320]{1,0:T(8,128)S(1)} fusion(s32[32,160]{1,0:T(8,128)} %param.19), kind=kLoop, calls=%fused_computation.12 | loop fusion | flops 4904960 | bytes 61440 | tf_op jit(solution)/shard_map/reduce_sum | solution.py:123
  22.7 5.3 %fusion.66 = (bf16[320,1,16,256]{3,2,1,0:T(8,128)(2,1)}, bf16[320,1,16,256]{3,2,1,0:T(8,128)(2,1)}) fusion(bf16[320,2,16,256]{3,2,1,0:T(8,128)(2,1)} %param.17), kind=kLoop, calls=%fused_computation.144 | loop fusion | bytes 10485760 | tf_op jit(solution)/shard_map/slice | solution.py:131
  27.9 0.7 fusion.19
  28.6 10.8 %psum.7 = bf16[64,96]{1,0:T(8,128)(2,1)S(1)} all-reduce(f32[64,96]{1,0:T(8,128)S(1)} %fusion.19), channel_id=1, replica_groups=mesh['groups'=2,'adapter'=4,'head'=4] {'head'}, use_global_device_ids=true, to_apply=%region_9.10 | all-reduce | flops 6144 | bytes 36864 | tf_op jit(solution)/shard_map/psum | solution.py:81
  41.0 0.8 fusion.20
  41.7 4.8 %all-to-all-start.1 = ((bf16[4,16,2560]{2,1,0:T(8,128)(2,1)}), bf16[4,16,2560]{2,1,0:T(8,128)(2,1)S(1)}, u32[]{:S(2)}, u32[]{:S(2)}) async-start(bf16[4,16,2560]{2,1,0:T(8,128)(2,1)} %fusion.20), calls=%async_computation.1 | async-start | bytes 655360 | tf_op jit(solution)/shard_map/all_to_all | solution.py:102
  47.0 1.1 fusion.9
  48.1 0.9 copy.57
  49.0 4.9 %reshape_squeeze.6 = bf16[5120,2,128]{2,1,0:T(2,128)(2,1)} reshape(bf16[320,1,16,256]{3,2,1,0:T(8,128)(2,1)} %get-tuple-element.12) | data formatting | bytes 5242880 | tf_op jit(solution)/shard_map/reshape;squeeze | solution.py:131
  53.9 4.9 %reshape_squeeze.7 = bf16[5120,2,128]{2,1,0:T(2,128)(2,1)} reshape(bf16[320,1,16,256]{3,2,1,0:T(8,128)(2,1)} %get-tuple-element.13) | data formatting | bytes 5242880 | tf_op jit(solution)/shard_map/reshape;squeeze | solution.py:132
  58.8 0.6 dynamic-slice
  60.2 0.7 gather_fusion.1
  61.3 4.6 %bitcast_reduce_fusion = (f32[32,2,8]{2,0,1:T(8,128)S(1)}, f32[2,32,8,5120]{3,2,1,0:T(8,128)S(1)}) fusion(pred[32,5120]{1,0:T(8,128)(4,1)S(1)} %copy.57, bf16[5120,2,128,1]{2,1,0,3:T(2,128)(2,1)} %bitcast.157, bf16[32,2,8,128]{3,2,1,0:T(8,128)(2,1)S(1)} %bitcast.166), kind=kOutput, calls=%fused_computation.5 | convolution fusion | flops 678952448 | bytes 13404160 | tf_op jit(solution)/shard_map/ikgd,tkd->ikgt/dot_general | solution.py:136
  65.9 3.0 %fusion.2 = f32[32,2,8]{2,0,1:T(8,128)S(1)} fusion(f32[2,32,8,5120]{3,2,1,0:T(8,128)S(1)} %get-tuple-element.25, f32[32,2,8]{2,0,1:T(8,128)S(1)} %fusion.41, pred[32,5120]{1,0:T(8,128)(4,1)S(1)} %copy.57), kind=kLoop, calls=%fused_computation.11 | loop fusion | flops 10485248 | bytes 10653696 | tf_op jit(solution)/shard_map/reduce_sum | solution.py:152
  69.0 3.5 %fusion.16 = bf16[32,2,8,128]{3,2,0,1:T(8,128)(2,1)S(1)} fusion(bf16[5120,2,128,1]{2,1,0,3:T(2,128)(2,1)S(1)} %bitcast.161, f32[2,32,8,5120]{3,2,1,0:T(8,128)S(1)} %get-tuple-element.25, f32[32,2,8]{2,0,1:T(8,128)S(1)} %get-tuple-element.17, f32[32,2,8]{2,0,1:T(8,128)S(1)} %fusion.41, pred[32,5120]{1,0:T(8,128)(4,1)S(1)} %copy.57, ...), kind=kOutput, calls=%fused_computation.26 | convolution fusion | flops 684392448 | bytes 13441024 | tf_op jit(solution)/shard_map/ikgt,tkd->ikgd/dot_general | solution.py:155
  72.6 15.6 %all_gather.3 = bf16[128,2048]{1,0:T(8,128)(2,1)S(1)} all-gather(bf16[32,2048]{1,0:T(8,128)(2,1)S(1)} %bitcast.167), channel_id=1, replica_groups=mesh['groups'=2,'adapter'=4,'head'=4] {'adapter'}, dimensions={0}, use_global_device_ids=true | all-gather | bytes 655360 | tf_op jit(solution)/shard_map/all_gather | solution.py:162
  88.2 0.7 gather_fusion.2
  88.9 1.4 fusion.22
  90.4 10.1 %all-reduce = bf16[64,32]{0,1:T(8,128)(2,1)S(1)} all-reduce(f32[64,32]{0,1:T(8,128)S(1)} %multiply_reduce_fusion), channel_id=2, replica_groups=mesh['groups'=2,'adapter'=4,'head'=4] {'head'}, use_global_device_ids=true, to_apply=%region_14.15.clone | all-reduce | flops 2048 | bytes 12288
  100.5 0.5 fusion.1
  101.0 1.4 copy.129
  102.4 5.4 %all-to-all-start.2 = ((f32[64,4,2048]{2,0,1:T(8,128)}), f32[64,4,2048]{2,0,1:T(8,128)}, u32[]{:S(2)}, u32[]{:S(2)}) async-start(f32[64,4,2048]{2,0,1:T(8,128)} %bitcast.158), calls=%async_computation.2 | async-start | bytes 4194304 | tf_op jit(solution)/shard_map/all_to_all | solution.py:179
  107.9 47.8 %all-to-all-done.2 = f32[64,4,2048]{2,0,1:T(8,128)} async-done(((f32[64,4,2048]{2,0,1:T(8,128)}), f32[64,4,2048]{2,0,1:T(8,128)}, u32[]{:S(2)}, u32[]{:S(2)}) %all-to-all-start.2) | async-done | bytes 2097184 | tf_op jit(solution)/shard_map/all_to_all | solution.py:179
  155.7 3.0 %gather_fusion.3 = f32[128,2048]{1,0:T(8,128)S(1)} fusion(f32[256,2048]{1,0:T(8,128)} %bitcast.35, s32[1024]{0:T(1024)S(1)} %pad_clamp_fusion), kind=kCustom, calls=%fused_computation.3 | custom fusion | bytes 2097664 | tf_op jit(solution)/shard_map/jit(_take)/gather | solution.py:186
  158.8 5.7 %convolution_add_fusion = f32[128,2048]{1,0:T(8,128)} fusion(bf16[128,2048]{1,0:T(8,128)(2,1)S(1)} %all_gather.3, bf16[2048,2048]{1,0:T(8,128)(2,1)} %param.27, f32[128,2048]{1,0:T(8,128)S(1)} %gather_fusion.3, pred[128]{0:T(512)(128)(4,1)S(1)} %get-tuple-element.7), kind=kOutput, calls=%fused_computation.22 | convolution fusion | flops 1074266112 | bytes 11010176 | tf_op jit(solution)/shard_map/dot_general | solution.py:163
  164.4 23.2 %reduce-scatter.2.cloned.1.call-done = f32[32,2048]{1,0:T(8,128)} async-done(((f32[128,2048]{1,0:T(8,128)}), f32[32,2048]{1,0:T(8,128)}) %reduce-scatter.2.cloned.1.call-update) | async-done | bytes 262160 | tf_op jit(solution)/shard_map/reduce_scatter | solution.py:188
  187.6 1.6 convert_element_type.108
  (77 shorter events, 3.7 us)
Async XLA Ops:
  6.5 21.4 %copy-start = (bf16[4,2048,96]{1,2,0:T(8,128)(2,1)S(1)}, bf16[4,2048,96]{1,2,0:T(8,128)(2,1)}, u32[]{:S(2)}) copy-start(bf16[4,2048,96]{1,2,0:T(8,128)(2,1)} %param.22) | copy-start | bytes 4718596
  11.1 16.8 %all-to-all-start = ((bf16[4,16,2048]{2,1,0:T(8,128)(2,1)}), bf16[4,16,2048]{2,1,0:T(8,128)(2,1)S(1)}, u32[]{:S(2)}, u32[]{:S(2)}) async-start(bf16[4,16,2048]{2,1,0:T(8,128)(2,1)} %select_select_fusion), calls=%async_computation | async-start | bytes 524288 | tf_op jit(solution)/shard_map/all_to_all | solution.py:70
  22.6 17.2 %copy-start.4 = (bf16[4,2,32,256]{3,2,1,0:T(8,128)(2,1)S(1)}, bf16[4,2,32,256]{3,2,1,0:T(8,128)(2,1)}, u32[]{:S(2)}) copy-start(bf16[4,2,32,256]{3,2,1,0:T(8,128)(2,1)} %param.24) | copy-start | bytes 393220
  22.6 18.1 %copy-start.2 = (bf16[4,32,2048]{2,1,0:T(8,128)(2,1)S(1)}, bf16[4,32,2048]{2,1,0:T(8,128)(2,1)}, u32[]{:S(2)}) copy-start(bf16[4,32,2048]{2,1,0:T(8,128)(2,1)} %param.23) | copy-start | bytes 1572868
  27.9 19.0 %copy-start.7 = (s32[32]{0:T(128)S(1)}, s32[32]{0:T(128)}, u32[]{:S(2)}) copy-start(s32[32]{0:T(128)} %param.18) | copy-start | bytes 388
  41.7 18.4 %all-to-all-start.1 = ((bf16[4,16,2560]{2,1,0:T(8,128)(2,1)}), bf16[4,16,2560]{2,1,0:T(8,128)(2,1)S(1)}, u32[]{:S(2)}, u32[]{:S(2)}) async-start(bf16[4,16,2560]{2,1,0:T(8,128)(2,1)} %fusion.20), calls=%async_computation.1 | async-start | bytes 655360 | tf_op jit(solution)/shard_map/all_to_all | solution.py:102
  49.0 9.9 %copy-start.8 = (u32[32]{0:T(128)S(1)}, u32[32]{0:T(128)}, u32[]{:S(2)}) copy-start(u32[32]{0:T(128)} %constant.129) | copy-start | bytes 388
  49.0 11.1 %copy-start.5 = (bf16[32,2,256]{2,1,0:T(2,128)(2,1)S(1)}, bf16[32,2,256]{2,1,0:T(2,128)(2,1)}, u32[]{:S(2)}) copy-start(bf16[32,2,256]{2,1,0:T(2,128)(2,1)} %param.16) | copy-start | bytes 98308
  49.0 11.9 %copy-start.6 = (bf16[32,2048]{1,0:T(8,128)(2,1)S(1)}, bf16[32,2048]{1,0:T(8,128)(2,1)}, u32[]{:S(2)}) copy-start(bf16[32,2048]{1,0:T(8,128)(2,1)} %param.15) | copy-start | bytes 393220
  65.9 3.1 %copy-start.1 = (bf16[5120,2,128]{2,1,0:T(2,128)(2,1)S(1)}, bf16[5120,2,128]{2,1,0:T(2,128)(2,1)}, u32[]{:S(2)}) copy-start(bf16[5120,2,128]{2,1,0:T(2,128)(2,1)} %reshape_squeeze.7) | copy-start | bytes 7864324
  69.0 31.5 %copy-start.3 = (bf16[4,8,8192]{2,1,0:T(8,128)(2,1)S(1)}, bf16[4,8,8192]{2,1,0:T(8,128)(2,1)}, u32[]{:S(2)}) copy-start(bf16[4,8,8192]{2,1,0:T(8,128)(2,1)} %param.26) | copy-start | bytes 1572868
  102.4 53.3 %all-to-all-start.2 = ((f32[64,4,2048]{2,0,1:T(8,128)}), f32[64,4,2048]{2,0,1:T(8,128)}, u32[]{:S(2)}, u32[]{:S(2)}) async-start(f32[64,4,2048]{2,0,1:T(8,128)} %bitcast.158), calls=%async_computation.2 | async-start | bytes 4194304 | tf_op jit(solution)/shard_map/all_to_all | solution.py:179
  107.8 79.8 %reduce-scatter.2.cloned.1.call-start = ((), (), s32[]{:S(2)}) async-start(), calls=%async_computation.4 | async-start | bytes 1310720 | tf_op jit(solution)/shard_map/reduce_scatter | solution.py:188
Sparse Core Ops, SparseCore 0:
  164.6 23.0 reduce-scatter.1
where the time goes:
time: 197 us; the launch traced here: 196 us
  waiting for transfers between devices  71 us (36%)
  blocking collectives  36.6 us (19%)
  local copies, waits for them, and re-layouts  25.7 us (13%)
  matrix products  17.7 us (9%)
  starting transfers between devices  16.5 us (8%)
  between operations  14.5 us (7%)
  other arithmetic  14.2 us (7%)
    all_to_all x1, waiting for transfers between devices, body(): lax.all_to_all(expanded_rows.reshape(spread, home_count, column_width), '...  47.8 us
    reduce_scatter x1, waiting for transfers between devices, body(): base_rows = lax.psum_scatter(terms, 'head', scatter_dimension=0, tiled=True)  23.2 us
    all_gather x1, blocking collectives, body(): every_attended = lax.all_gather(attended, 'adapter', axis=0, tiled=True)  15.6 us
    psum x1, blocking collectives, body(): rank_values = lax.psum(partial_value, 'head').astype(jnp.bfloat16)  10.8 us
    unnamed x1, blocking collectives  10.1 us
    all_to_all x1, starting transfers between devices, body(): lax.all_to_all(outgoing.reshape(home_count, slot_count, -1), 'adapter', s...  6.32 us
    dot_general x1, matrix products, body(): jnp.dot(every_attended, output_weight_matrix, preferred_element_type=jnp....  5.65 us
    all_to_all x1, starting transfers between devices, body(): lax.all_to_all(expanded_rows.reshape(spread, home_count, column_width), '...  5.38 us
  transfers between devices with their start and end apart: 4, of which 2 were waited for; matrix products, arithmetic and copies ran while one was open for 12% of the time, Pallas kernels for 0%

commit v1 on v0

v1 whole, which is shorter than its diff:
```python
import functools
import math

import jax
import jax.numpy as jnp
from jax import lax
from jax.experimental import pallas as pl
from jax.experimental.pallas import tpu as pltpu
from jax.sharding import PartitionSpec as P

QH = 64
KVH = 8
HD = 128
BF = jnp.bfloat16
F32 = jnp.float32
I32 = jnp.int32
CHUNK_PAGES = 64


def iota(shape, dim):
    return lax.broadcasted_iota(I32, shape, dim)


def mm(a, b, dims=((1,), (0,))):
    return lax.dot_general(a, b, (dims, ((), ())), preferred_element_type=F32)


def kernel(
    cfg,
    hid_ref, bq_ref, bkv_ref, len_ref, table_ref, plan_ref, reqad_ref,
    cache_hbm, down_hbm, qup_hbm, kvup_hbm, odown_hbm, oup_hbm, w_hbm,
    out_ref,
    cache_v, down_v, qup_v, kvup_v, odown_v, w_v,
    row_out, row_in, ps_out, ps_in, dl_out, dl_in, up_all, odc,
    bias_s, score_s, att, tot, rr_out, rr_in, ag, fin_out, fin_in,
    lsem, row_ss, row_rs, ps_ss, ps_rs, dl_ss, dl_rs, up_ss, up_rs,
    att_ss, att_rs, rr_ss, rr_rs, ag_ss, ag_rs, fin_ss, fin_rs,
):
    n, nh, rows, slot, na, rank = cfg
    total = n * rows
    cells = n * slot
    group = QH // KVH
    kvl = bkv_ref.shape[2] // HD
    half = group * HD
    qw = kvl * half
    kvw = kvl * HD
    z = lax.axis_index("adapter")
    h = lax.axis_index("head")

    def peer_z(d):
        return lax.rem(z + d, n)

    def peer_h(d):
        return lax.rem(h + d, nh)

    def rcopy(src, dst, ss, rs, axis, dev):
        return pltpu.make_async_remote_copy(
            src_ref=src, dst_ref=dst, send_sem=ss, recv_sem=rs,
            device_id={axis: dev}, device_id_type=pl.DeviceIdType.MESH,
        )

    locals_ = []
    for i, (src, dst) in enumerate((
        (down_hbm, down_v), (qup_hbm, qup_v), (kvup_hbm, kvup_v),
        (cache_hbm, cache_v), (odown_hbm, odown_v), (w_hbm, w_v),
    )):
        cp = pltpu.make_async_copy(src, dst, lsem.at[i])
        cp.start()
        locals_.append(cp)
    own_up = pltpu.make_async_copy(
        oup_hbm.at[:, pl.ds(pl.multiple_of(z * w_v.shape[1], 128), w_v.shape[1])],
        up_all.at[z], lsem.at[6])
    own_up.start()

    barrier = pltpu.get_barrier_semaphore()
    for d in range(1, n):
        pl.semaphore_signal(barrier, inc=1, device_id={"adapter": peer_z(d)},
                            device_id_type=pl.DeviceIdType.MESH)
    for d in range(1, nh):
        pl.semaphore_signal(barrier, inc=1, device_id={"head": peer_h(d)},
                            device_id_type=pl.DeviceIdType.MESH)

    jj = iota((total, total), 0)
    ii = iota((total, total), 1)
    eye = jj == ii

    def to_col(row):
        return jnp.sum(jnp.where(eye, row, 0), axis=1, keepdims=True)

    def to_row(col):
        return jnp.sum(jnp.where(eye, col, 0), axis=0, keepdims=True)

    plan_col = to_col(plan_ref[...])
    ad_col = jnp.sum(jnp.where(plan_col == ii, reqad_ref[...], 0), axis=1, keepdims=True)
    ad_row = to_row(ad_col)
    own_col = ad_col // na
    own_row = ad_row // na
    before = (own_col == own_row) & (jj // rows == ii // rows) & (ii < jj)
    slot_col = jnp.sum(before.astype(I32), axis=1, keepdims=True)
    slot_row = to_row(slot_col)
    target_col = own_col * slot + slot_col
    mine = iota((total, rows), 0) == z * rows + iota((total, rows), 1)
    my_target = jnp.sum(jnp.where(mine, target_col, 0), axis=0, keepdims=True)
    give = (my_target == iota((cells, rows), 0)).astype(F32).astype(BF)
    place_row = (iota((1, total), 1) // rows) * slot + slot_row
    cell_hit = (own_row == z) & (place_row == iota((cells, total), 0))
    local_ad = jnp.sum(jnp.where(cell_hit, ad_row - own_row * na + 1, 0), axis=1, keepdims=True) - 1

    outgoing = mm(give, hid_ref[...]).astype(BF)
    row_out[...] = outgoing.reshape(row_out.shape)
    row_in[z] = row_out[z]

    pl.semaphore_wait(barrier, n - 1 + nh - 1)

    sends = []
    for d in range(1, n):
        o = peer_z(d)
        cp = rcopy(row_out.at[o], row_in.at[z], row_ss.at[o], row_rs.at[z], "adapter", o)
        cp.start()
        sends.append(cp)

    pages = cache_v.shape[0]
    page_len = cache_v.shape[2]
    ct = CHUNK_PAGES * page_len
    nchunk = pages // CHUNK_PAGES
    table = table_ref[...]
    page_ids = iota((rows, pages), 1)
    pos = jnp.zeros((rows, pages), I32)
    for t in range(table.shape[1]):
        pos = jnp.where(table[:, t:t + 1] == page_ids, t + 1, pos)
    len_col = jnp.sum(jnp.where(iota((rows, rows), 0) == iota((rows, rows), 1), len_ref[...], 0),
                      axis=1, keepdims=True)
    lim = jnp.where(pos > 0, jnp.clip(len_col - page_len * (pos - 1), 0, page_len), 0)
    lim = lim.astype(F32).astype(BF)
    spread = (iota((CHUNK_PAGES, ct), 1) // page_len == iota((CHUNK_PAGES, ct), 0)).astype(F32).astype(BF)
    within_page = lax.rem(iota((rows, ct), 1), page_len).astype(F32)
    for c in range(nchunk):
        wide = mm(lim[:, c * CHUNK_PAGES:(c + 1) * CHUNK_PAGES], spread)
        bias_s[c] = jnp.where(within_page < wide, 0.0, -jnp.inf)
    locals_[4].wait()
    for a in range(na):
        odc[:, a * rank:(a + 1) * rank] = odown_v[a]

    locals_[0].wait()
    for d in range(1, n):
        o = peer_z(d)
        rcopy(row_out.at[o], row_in.at[o], row_ss.at[o], row_rs.at[o], "adapter", o).wait_recv()

    received = row_in[...].reshape(cells, row_in.shape[2])
    part = jnp.zeros((cells, 3 * rank), F32)
    for a in range(na):
        part = jnp.where(local_ad == a, mm(received, down_v[a]), part)
    ps_out[...] = part
    for d in range(1, nh):
        p = peer_h(d)
        cp = rcopy(ps_out, ps_in.at[h], ps_ss.at[p], ps_rs.at[h], "head", p)
        cp.start()
        sends.append(cp)
    cols = w_v.shape[1]
    for d in range(1, n):
        o = peer_z(d)
        cp = rcopy(oup_hbm.at[:, pl.ds(pl.multiple_of(o * cols, 128), cols)], up_all.at[z],
                   up_ss.at[o], up_rs.at[z], "adapter", o)
        cp.start()
        sends.append(cp)
    locals_[1].wait()
    locals_[2].wait()
    for d in range(1, nh):
        p = peer_h(d)
        rcopy(ps_out, ps_in.at[p], ps_ss.at[p], ps_rs.at[p], "head", p).wait_recv()
        part = part + ps_in[p]
    part = part * 0.5

    def chosen(lo):
        piece = part[:, lo:lo + rank]
        return jnp.concatenate(
            [jnp.where(local_ad == a, piece, 0.0) for a in range(na)], axis=1).astype(BF)

    dl_out[:, :, :qw] = mm(chosen(0), qup_v[...]).astype(BF).reshape(n, slot, qw)
    for i in range(2):
        maps = jnp.concatenate([kvup_v[a, i] for a in range(na)], axis=0)
        dl_out[:, :, qw + i * kvw:qw + (i + 1) * kvw] = (
            mm(chosen((1 + i) * rank), maps).astype(BF).reshape(n, slot, kvw))
    dl_in[z] = dl_out[z]
    for d in range(1, n):
        o = peer_z(d)
        cp = rcopy(dl_out.at[o], dl_in.at[z], dl_ss.at[o], dl_rs.at[z], "adapter", o)
        cp.start()
        sends.append(cp)
    eye_r = (iota((rows, total), 0) + z * rows) == iota((rows, total), 1)
    target_row = own_row * slot + slot_row
    take_col = jnp.sum(jnp.where(eye_r, target_row, 0), axis=1, keepdims=True)
    take = (take_col == iota((rows, cells), 1)).astype(F32).astype(BF)
    locals_[3].wait()
    for d in range(1, n):
        o = peer_z(d)
        rcopy(dl_out.at[o], dl_in.at[o], dl_ss.at[o], dl_rs.at[o], "adapter", o).wait_recv()
    delta = mm(take, dl_in[...].reshape(cells, dl_in.shape[2]))
    query = (bq_ref[...].astype(F32) + delta[:, :qw]).astype(BF)
    key_new = (bkv_ref[:, 0, :].astype(F32) + delta[:, qw:qw + kvw]).astype(BF).astype(F32)
    value_new = (bkv_ref[:, 1, :].astype(F32) + delta[:, qw + kvw:]).astype(BF).astype(F32)

    scale = HD ** -0.5 * math.log2(math.e)
    gr = group * rows
    for k in range(kvl):
        lanes = slice(k * HD, (k + 1) * HD)
        qh = jnp.concatenate(
            [query[:, k * half + g * HD:k * half + (g + 1) * HD] for g in range(group)], axis=0)
        kn = jnp.concatenate([key_new[:, lanes]] * group, axis=0)
        vn = jnp.concatenate([value_new[:, lanes]] * group, axis=0)
        own = jnp.sum(qh.astype(F32) * kn, axis=1, keepdims=True) * scale

        def scores(c, top):
            keys = cache_v[pl.ds(c * CHUNK_PAGES, CHUNK_PAGES), 0, :, lanes].reshape(ct, HD)
            s = mm(qh, keys, ((1,), (1,))) * scale
            s = (s.reshape(group, rows, ct) + bias_s[c][None]).reshape(gr, ct)
            score_s[c] = s
            for i in range(ct // HD):
                top = jnp.maximum(top, s[:, i * HD:(i + 1) * HD])
            return top

        top = lax.fori_loop(0, nchunk, scores, jnp.full((gr, HD), -jnp.inf, F32))
        top = jnp.maximum(jnp.max(top, axis=1, keepdims=True), own)

        def mix(c, carry):
            acc, den = carry
            w = jnp.exp2(score_s[c] - top)
            for i in range(ct // HD):
                den = den + w[:, i * HD:(i + 1) * HD]
            values = cache_v[pl.ds(c * CHUNK_PAGES, CHUNK_PAGES), 1, :, lanes].reshape(ct, HD)
            return acc + mm(w.astype(BF), values), den

        zero = jnp.zeros((gr, HD), F32)
        acc, den = lax.fori_loop(0, nchunk, mix, (zero, zero))
        own_w = jnp.exp2(own - top)
        den = jnp.sum(den, axis=1, keepdims=True) + own_w
        mixed = ((acc + own_w * vn) / den).astype(BF)
        for g in range(group):
            att[k, z, :, g * HD:(g + 1) * HD] = mixed[g * rows:(g + 1) * rows]
        for d in range(1, n):
            o = peer_z(d)
            cp = rcopy(att.at[k, z], att.at[k, z], att_ss.at[k, o], att_rs.at[k, z], "adapter", o)
            cp.start()
            sends.append(cp)

    locals_[5].wait()
    nc, _, cw = tot.shape
    racc = jnp.zeros((total, na * rank), F32)
    for k in range(kvl):
        for d in range(1, n):
            o = peer_z(d)
            rcopy(att.at[k, o], att.at[k, o], att_ss.at[k, o], att_rs.at[k, o], "adapter", o).wait_recv()
        every = att[k].reshape(total, half)
        racc = racc + mm(every, odc[k * half:(k + 1) * half])
        if k == kvl - 1:
            turned = racc.T
            turned = jnp.where(ad_row == z * na + iota((na * rank, total), 0) // rank, turned, 0.0)
            ranks = turned[:rank]
            for a in range(1, na):
                ranks = ranks + turned[a * rank:(a + 1) * rank]
            rl = rank // nh
            for p in range(nh):
                rr_out[p] = ranks[p * rl:(p + 1) * rl]
            for d in range(1, nh):
                p = peer_h(d)
                cp = rcopy(rr_out.at[p], rr_in.at[h], rr_ss.at[p], rr_rs.at[h], "head", p)
                cp.start()
                sends.append(cp)
        for c in range(nc):
            term = mm(every, w_v[k * half:(k + 1) * half, c * cw:(c + 1) * cw])
            if k == 0:
                tot[c] = term
            else:
                tot[c] = tot[c] + term
            if k == kvl - 1 and c == 0:
                summed = rr_out[h]
                for d in range(1, nh):
                    p = peer_h(d)
                    rcopy(rr_out.at[p], rr_in.at[p], rr_ss.at[p], rr_rs.at[p], "head", p).wait_recv()
                    summed = summed + rr_in[p]
                ag[z] = summed
                for d in range(1, n):
                    o = peer_z(d)
                    cp = rcopy(ag.at[z], ag.at[z], ag_ss.at[o], ag_rs.at[z], "adapter", o)
                    cp.start()
                    sends.append(cp)

    for d in range(1, n):
        o = peer_z(d)
        rcopy(ag.at[o], ag.at[o], ag_ss.at[o], ag_rs.at[o], "adapter", o).wait_recv()
        rcopy(oup_hbm.at[:, pl.ds(pl.multiple_of(o * cols, 128), cols)], up_all.at[o],
              up_ss.at[o], up_rs.at[o], "adapter", o).wait_recv()
    own_up.wait()
    mine_ranks = ag[0]
    for o in range(1, n):
        mine_ranks = mine_ranks + ag[o]
    rl = rank // nh
    kk = n * na * rl
    tile = (lax.rem(iota((rl, kk), 1), rl) == iota((rl, kk), 0)).astype(F32).astype(BF)
    sel = mm(mine_ranks.astype(BF), tile, ((0,), (0,)))
    sel = jnp.where(ad_col == iota((total, kk), 1) // rl, sel * 0.5, 0.0).astype(BF)
    out_rows = total // nh
    for c in range(nc):
        ups = up_all[:, :, c * cw:(c + 1) * cw].reshape(kk, cw)
        full = tot[c] + mm(sel, ups)
        tot[c] = full
        fin_out[c] = full.astype(BF).reshape(nh, out_rows, cw)
        for d in range(1, nh):
            p = peer_h(d)
            cp = rcopy(fin_out.at[c, p], fin_in.at[c, h], fin_ss.at[c, p], fin_rs.at[c, h], "head", p)
            cp.start()
            sends.append(cp)
    for c in range(nc):
        res = tot[c, pl.ds(pl.multiple_of(h * out_rows, 8), out_rows), :]
        for d in range(1, nh):
            p = peer_h(d)
            rcopy(fin_out.at[c, p], fin_in.at[c, p], fin_ss.at[c, p], fin_rs.at[c, p], "head", p).wait_recv()
            res = res + fin_in[c, p].astype(F32)
        out_ref[:, c * cw:(c + 1) * cw] = res.astype(BF)
    for cp in sends:
        cp.wait_send()


def body(
    normed_hidden_rows,
    base_query,
    base_key_value,
    key_value_cache,
    cached_length_per_request,
    request_page_table,
    planned_request_rows,
    request_adapters,
    query_key_value_down_maps,
    query_up_maps,
    key_value_up_maps,
    output_down_maps,
    output_up_maps,
    output_weight_matrix,
):
    n = lax.axis_size("adapter")
    nh = lax.axis_size("head")
    rows, feats = normed_hidden_rows.shape
    total = planned_request_rows.shape[0]
    na, _, rank = output_down_maps.shape
    slot = max(16, 2 * rows // n)
    cells = n * slot
    qw = base_query.shape[1]
    kvw = base_key_value.shape[2]
    kvl = kvw // HD
    half = qw // kvl
    dw = qw + 2 * kvw
    cols = output_weight_matrix.shape[1]
    cw = min(512, cols)
    nc = cols // cw
    pages, _, page_len, _ = key_value_cache.shape
    ct = CHUNK_PAGES * page_len
    gr = QH // KVH * rows
    out_rows = total // nh
    rl = rank // nh
    vm = pl.BlockSpec(memory_space=pltpu.VMEM)
    hb = pl.BlockSpec(memory_space=pl.ANY)
    dma = pltpu.SemaphoreType.DMA
    ups = output_up_maps.reshape(na * output_up_maps.shape[1], -1)
    qups = query_up_maps.reshape(na * rank, qw)
    return pl.pallas_call(
        functools.partial(kernel, (n, nh, rows, slot, na, rank)),
        out_shape=jax.ShapeDtypeStruct((out_rows, cols), BF),
        in_specs=[vm] * 7 + [hb] * 7,
        out_specs=vm,
        scratch_shapes=[
            pltpu.VMEM(key_value_cache.shape, BF),
            pltpu.VMEM(query_key_value_down_maps.shape, BF),
            pltpu.VMEM(qups.shape, BF),
            pltpu.VMEM(key_value_up_maps.shape, BF),
            pltpu.VMEM(output_down_maps.shape, BF),
            pltpu.VMEM(output_weight_matrix.shape, BF),
            pltpu.VMEM((n, slot, feats), BF),
            pltpu.VMEM((n, slot, feats), BF),
            pltpu.VMEM((cells, 3 * rank), F32),
            pltpu.VMEM((nh, cells, 3 * rank), F32),
            pltpu.VMEM((n, slot, dw), BF),
            pltpu.VMEM((n, slot, dw), BF),
            pltpu.VMEM((n, ups.shape[0], cols), BF),
            pltpu.VMEM((output_down_maps.shape[1], na * rank), BF),
            pltpu.VMEM((pages // CHUNK_PAGES, rows, ct), F32),
            pltpu.VMEM((pages // CHUNK_PAGES, gr, ct), F32),
            pltpu.VMEM((kvl, n, rows, half), BF),
            pltpu.VMEM((nc, total, cw), F32),
            pltpu.VMEM((nh, rl, total), F32),
            pltpu.VMEM((nh, rl, total), F32),
            pltpu.VMEM((n, rl, total), F32),
            pltpu.VMEM((nc, nh, out_rows, cw), BF),
            pltpu.VMEM((nc, nh, out_rows, cw), BF),
            dma((7,)),
            dma((n,)), dma((n,)),
            dma((nh,)), dma((nh,)),
            dma((n,)), dma((n,)),
            dma((n,)), dma((n,)),
            dma((kvl, n)), dma((kvl, n)),
            dma((nh,)), dma((nh,)),
            dma((n,)), dma((n,)),
            dma((nc, nh)), dma((nc, nh)),
        ],
        compiler_params=pltpu.CompilerParams(
            collective_id=0, has_side_effects=True, vmem_limit_bytes=58 * 1024 * 1024),
    )(
        normed_hidden_rows, base_query, base_key_value,
        cached_length_per_request.reshape(1, rows), request_page_table,
        planned_request_rows.reshape(1, total), request_adapters.reshape(1, total),
        key_value_cache, query_key_value_down_maps, qups, key_value_up_maps,
        output_down_maps, ups, output_weight_matrix,
    )


def solution(mesh):
    return jax.shard_map(
        body,
        mesh=mesh,
        in_specs=(
            P(("groups", "adapter"), "head"),
            P(("groups", "adapter"), "head"),
            P(("groups", "adapter"), None, "head"),
            P(("groups", "adapter"), None, None, "head"),
            P(("groups", "adapter")),
            P(("groups", "adapter"), None),
            P("groups"),
            P("groups"),
            P("adapter", "head", None),
            P("adapter", None, "head"),
            P("adapter", None, None, "head"),
            P("adapter", "head", None),
            P("adapter", "head", None),
            P("head", "adapter"),
        ),
        out_specs=P(("groups", "head"), "adapter"),
        check_vma=False,
    )
```

time: 197 us -> 71.4 us (0.36)
  waiting for transfers between devices: 71 us -> 0 us
  Pallas kernels: 0 us -> 64.1 us
  blocking collectives: 36.6 us -> 0 us
  local copies, waits for them, and re-layouts: 25.7 us -> 7.1 us
  matrix products: 17.7 us -> 0 us
  starting transfers between devices: 16.5 us -> 0 us
  between operations: 14.5 us -> 0.01 us
  other arithmetic: 14.2 us -> 0 us
    pallas_call x0 -> x1, Pallas kernels: none -> 64.1 us  [body(): pl.pallas_call(functools.partial(kernel, (n, nh, rows, slot, na, rank)),...]
    all_to_all x3 -> x0, waiting for transfers between devices: 47.8 us -> none  [the longest x1 47.8 us: body(): lax.all_to_all(expanded_rows.reshape(spread, home_count, column_width), '...]
    reduce_scatter x1 -> x0, waiting for transfers between devices: 23.2 us -> none  [body(): base_rows = lax.psum_scatter(terms, 'head', scatter_dimension=0, tiled=True)]
    all_to_all x3 -> x0, starting transfers between devices: 16.5 us -> none  [the longest x1 6.32 us: body(): lax.all_to_all(outgoing.reshape(home_count, slot_count, -1), 'adapter', s...]
    dot_general x9 -> x0, matrix products: 16.3 us -> none  [the longest x1 5.65 us: body(): jnp.dot(every_attended, output_weight_matrix, preferred_element_type=jnp....]
    all_gather x1 -> x0, blocking collectives: 15.6 us -> none  [body(): every_attended = lax.all_gather(attended, 'adapter', axis=0, tiled=True)]
    psum x1 -> x0, blocking collectives: 10.8 us -> none  [body(): rank_values = lax.psum(partial_value, 'head').astype(jnp.bfloat16)]
    unnamed x1 -> x0, blocking collectives: 10.1 us -> none
  transfers between devices with their start and end apart: 4 -> 0, of which waited for: 2 -> 0; matrix products, arithmetic and copies ran while one was open for 12% -> 0% of each run, Pallas kernels for 0% -> 0%
where the time goes in v1:
time: 71.4 us; the launch traced here: 71.2 us
  Pallas kernels  64.1 us (90%)
  local copies, waits for them, and re-layouts  7.1 us (10%)
    pallas_call x1, Pallas kernels, body(): pl.pallas_call(functools.partial(kernel, (n, nh, rows, slot, na, rank)),...  64.1 us
    unnamed x5, local copies, waits for them, and re-layouts  7.1 us

profile of v1, /device:TPU:0, one launch (start us, length us, event | category | flops | bytes accessed | tf_op | source)
XLA Modules:
  0.0 71.2 jit_solution(5324748219342566157)
XLA Ops:
  0.0 0.0 copy-start
  0.0 3.8 %copy.15.down_hbm = bf16[4,2048,96]{2,1,0:T(8,128)(2,1)} copy(bf16[4,2048,96]{1,2,0:T(8,128)(2,1)} %param.22) | data formatting | bytes 3145728 | tf_op args[8]
  3.8 0.0 copy-done
  3.8 1.7 %copy.16.odown_hbm = bf16[4,2048,32]{2,1,0:T(8,128)(2,1)} copy(bf16[4,2048,32]{1,2,0:T(8,128)(2,1)S(1)} %copy-done) | data formatting | bytes 1048576 | tf_op args[11]
  5.5 64.1 %shard_map.136 = bf16[32,2048]{1,0:T(8,128)(2,1)} custom-call(bf16[32,2048]{1,0:T(8,128)(2,1)} %hid_ref.1, bf16[32,2048]{1,0:T(8,128)(2,1)} %bq_ref.1, bf16[32,2,256]{2,1,0:T(2,128)(2,1)} %bkv_ref.1, s32[1,32]{1,0:T(1,128)} %bitcast.7, s32[32,160]{1,0:T(8,128)} %table_ref.1, s32[1,128]{1,0:T(1,128)} %bitcast.8, s32[1,128]{1,0:T(1,128)} %bitcast.9, ...), custom_call_target="tpu_custom_call" | custom-call | tf_op jit(solution)/shard_map/pallas_call | solution.py:365
  69.7 1.6 %copy.18 = bf16[32,2048]{1,0:T(8,128)(2,1)} copy(bf16[32,2048]{1,0:T(8,128)(2,1)} %shard_map.136) | data formatting | bytes 262144
Async XLA Ops:
  0.0 3.8 %copy-start = (bf16[4,2048,32]{1,2,0:T(8,128)(2,1)S(1)}, bf16[4,2048,32]{1,2,0:T(8,128)(2,1)}, u32[]{:S(2)}) copy-start(bf16[4,2048,32]{1,2,0:T(8,128)(2,1)} %param.25) | copy-start | bytes 1572868

commit v2 on v1

--- a/solution.py
+++ b/solution.py
@@ -31,10 +31,10 @@
     cache_hbm, down_hbm, qup_hbm, kvup_hbm, odown_hbm, oup_hbm, w_hbm,
     out_ref,
     cache_v, down_v, qup_v, kvup_v, odown_v, w_v,
-    row_out, row_in, ps_out, ps_in, dl_out, dl_in, up_all, odc,
-    bias_s, score_s, att, tot, rr_out, rr_in, ag, fin_out, fin_in,
+    row_out, row_in, ps_out, ps_in, dl_out, dl_in, up_all,
+    bias_s, score_s, att, tot, rr_out, rr_in, fin_out, fin_in,
     lsem, row_ss, row_rs, ps_ss, ps_rs, dl_ss, dl_rs, up_ss, up_rs,
-    att_ss, att_rs, rr_ss, rr_rs, ag_ss, ag_rs, fin_ss, fin_rs,
+    y_ss, y_rs, att_ss, att_rs, rr_ss, rr_rs, fin_ss, fin_rs,
 ):
     n, nh, rows, slot, na, rank = cfg
     total = n * rows
@@ -43,9 +43,12 @@
     kvl = bkv_ref.shape[2] // HD
     half = group * HD
     qw = kvl * half
-    kvw = kvl * HD
     z = lax.axis_index("adapter")
     h = lax.axis_index("head")
+    gi = lax.axis_index("groups")
+    ng = lax.axis_size("groups")
+    me = z * nh + h
+    plane = n * nh
 
     def peer_z(d):
         return lax.rem(z + d, n)
@@ -56,7 +59,7 @@
     def rcopy(src, dst, ss, rs, axis, dev):
         return pltpu.make_async_remote_copy(
             src_ref=src, dst_ref=dst, send_sem=ss, recv_sem=rs,
-            device_id={axis: dev}, device_id_type=pl.DeviceIdType.MESH,
+            device_id=dev if axis is None else {axis: dev}, device_id_type=pl.DeviceIdType.MESH,
         )
 
     locals_ = []
@@ -73,11 +76,18 @@
     own_up.start()
 
     barrier = pltpu.get_barrier_semaphore()
-    for d in range(1, n):
-        pl.semaphore_signal(barrier, inc=1, device_id={"adapter": peer_z(d)},
+
+    def plane_dev(d):
+        other = lax.rem(me + d, plane)
+        return other, {"adapter": other // nh, "head": lax.rem(other, nh)}
+
+    @pl.loop(1, plane)
+    def _(d):
+        pl.semaphore_signal(barrier, inc=1, device_id=plane_dev(d)[1],
                             device_id_type=pl.DeviceIdType.MESH)
-    for d in range(1, nh):
-        pl.semaphore_signal(barrier, inc=1, device_id={"head": peer_h(d)},
+
+    for d in range(1, ng):
+        pl.semaphore_signal(barrier, inc=1, device_id={"groups": lax.rem(gi + d, ng)},
                             device_id_type=pl.DeviceIdType.MESH)
 
     jj = iota((total, total), 0)
@@ -110,7 +120,7 @@
     row_out[...] = outgoing.reshape(row_out.shape)
     row_in[z] = row_out[z]
 
-    pl.semaphore_wait(barrier, n - 1 + nh - 1)
+    pl.semaphore_wait(barrier, plane - 1 + ng - 1)
 
     sends = []
     for d in range(1, n):
@@ -137,9 +147,6 @@
     for c in range(nchunk):
         wide = mm(lim[:, c * CHUNK_PAGES:(c + 1) * CHUNK_PAGES], spread)
         bias_s[c] = jnp.where(within_page < wide, 0.0, -jnp.inf)
-    locals_[4].wait()
-    for a in range(na):
-        odc[:, a * rank:(a + 1) * rank] = odown_v[a]
 
     locals_[0].wait()
     for d in range(1, n):
@@ -147,9 +154,10 @@
         rcopy(row_out.at[o], row_in.at[o], row_ss.at[o], row_rs.at[o], "adapter", o).wait_recv()
 
     received = row_in[...].reshape(cells, row_in.shape[2])
+    spread_ranks = mm(received, down_v[...], ((1,), (1,)))
     part = jnp.zeros((cells, 3 * rank), F32)
     for a in range(na):
-        part = jnp.where(local_ad == a, mm(received, down_v[a]), part)
+        part = jnp.where(local_ad == a, spread_ranks[:, a * 3 * rank:(a + 1) * 3 * rank], part)
     ps_out[...] = part
     for d in range(1, nh):
         p = peer_h(d)
@@ -157,10 +165,17 @@
         cp.start()
         sends.append(cp)
     cols = w_v.shape[1]
+    share = cols // ng
+
+    def up_src(o):
+        return oup_hbm.at[:, pl.ds(pl.multiple_of(o * cols + gi * share, 128), share)]
+
+    def up_part(o, who):
+        return up_all.at[o, :, pl.ds(pl.multiple_of(who * share, 128), share)]
+
     for d in range(1, n):
         o = peer_z(d)
-        cp = rcopy(oup_hbm.at[:, pl.ds(pl.multiple_of(o * cols, 128), cols)], up_all.at[z],
-                   up_ss.at[o], up_rs.at[z], "adapter", o)
+        cp = rcopy(up_src(o), up_part(z, gi), up_ss.at[o], up_rs.at[z], "adapter", o)
         cp.start()
         sends.append(cp)
     locals_[1].wait()
@@ -176,38 +191,50 @@
         return jnp.concatenate(
             [jnp.where(local_ad == a, piece, 0.0) for a in range(na)], axis=1).astype(BF)
 
-    dl_out[:, :, :qw] = mm(chosen(0), qup_v[...]).astype(BF).reshape(n, slot, qw)
-    for i in range(2):
-        maps = jnp.concatenate([kvup_v[a, i] for a in range(na)], axis=0)
-        dl_out[:, :, qw + i * kvw:qw + (i + 1) * kvw] = (
-            mm(chosen((1 + i) * rank), maps).astype(BF).reshape(n, slot, kvw))
-    dl_in[z] = dl_out[z]
-    for d in range(1, n):
-        o = peer_z(d)
-        cp = rcopy(dl_out.at[o], dl_in.at[z], dl_ss.at[o], dl_rs.at[z], "adapter", o)
-        cp.start()
-        sends.append(cp)
+    q_sel = chosen(0)
+    kv_sel = [chosen((1 + i) * rank) for i in range(2)]
+    for k in range(kvl):
+        dl_out[k, :, :, :half] = (
+            mm(q_sel, qup_v[:, k * half:(k + 1) * half]).astype(BF).reshape(n, slot, half))
+        for i in range(2):
+            maps = jnp.concatenate(
+                [kvup_v[a, i, :, k * HD:(k + 1) * HD] for a in range(na)], axis=0)
+            dl_out[k, :, :, half + i * HD:half + (i + 1) * HD] = (
+                mm(kv_sel[i], maps).astype(BF).reshape(n, slot, HD))
+        dl_in[k, z] = dl_out[k, z]
+        for d in range(1, n):
+            o = peer_z(d)
+            cp = rcopy(dl_out.at[k, o], dl_in.at[k, z], dl_ss.at[k, o], dl_rs.at[k, z], "adapter", o)
+            cp.start()
+            sends.append(cp)
     eye_r = (iota((rows, total), 0) + z * rows) == iota((rows, total), 1)
     target_row = own_row * slot + slot_row
     take_col = jnp.sum(jnp.where(eye_r, target_row, 0), axis=1, keepdims=True)
     take = (take_col == iota((rows, cells), 1)).astype(F32).astype(BF)
-    locals_[3].wait()
     for d in range(1, n):
         o = peer_z(d)
-        rcopy(dl_out.at[o], dl_in.at[o], dl_ss.at[o], dl_rs.at[o], "adapter", o).wait_recv()
-    delta = mm(take, dl_in[...].reshape(cells, dl_in.shape[2]))
-    query = (bq_ref[...].astype(F32) + delta[:, :qw]).astype(BF)
-    key_new = (bkv_ref[:, 0, :].astype(F32) + delta[:, qw:qw + kvw]).astype(BF).astype(F32)
-    value_new = (bkv_ref[:, 1, :].astype(F32) + delta[:, qw + kvw:]).astype(BF).astype(F32)
+        rcopy(up_src(o), up_part(o, gi), up_ss.at[o], up_rs.at[o], "adapter", o).wait_recv()
+        for e in range(1, ng):
+            y = lax.rem(gi + e, ng)
+            cp = rcopy(up_part(o, gi), up_part(o, gi), y_ss.at[y, o], y_rs.at[gi, o], "groups", y)
+            cp.start()
+            sends.append(cp)
+    locals_[3].wait()
 
     scale = HD ** -0.5 * math.log2(math.e)
     gr = group * rows
     for k in range(kvl):
         lanes = slice(k * HD, (k + 1) * HD)
-        qh = jnp.concatenate(
-            [query[:, k * half + g * HD:k * half + (g + 1) * HD] for g in range(group)], axis=0)
-        kn = jnp.concatenate([key_new[:, lanes]] * group, axis=0)
-        vn = jnp.concatenate([value_new[:, lanes]] * group, axis=0)
+        for d in range(1, n):
+            o = peer_z(d)
+            rcopy(dl_out.at[k, o], dl_in.at[k, o], dl_ss.at[k, o], dl_rs.at[k, o], "adapter", o).wait_recv()
+        delta = mm(take, dl_in[k].reshape(cells, dl_in.shape[3]))
+        query = (bq_ref[:, k * half:(k + 1) * half].astype(F32) + delta[:, :half]).astype(BF)
+        key_new = (bkv_ref[:, 0, lanes].astype(F32) + delta[:, half:half + HD]).astype(BF).astype(F32)
+        value_new = (bkv_ref[:, 1, lanes].astype(F32) + delta[:, half + HD:]).astype(BF).astype(F32)
+        qh = jnp.concatenate([query[:, g * HD:(g + 1) * HD] for g in range(group)], axis=0)
+        kn = jnp.concatenate([key_new] * group, axis=0)
+        vn = jnp.concatenate([value_new] * group, axis=0)
         own = jnp.sum(qh.astype(F32) * kn, axis=1, keepdims=True) * scale
 
         def scores(c, top):
@@ -243,17 +270,17 @@
             cp.start()
             sends.append(cp)
 
+    locals_[4].wait()
     locals_[5].wait()
     nc, _, cw = tot.shape
-    racc = jnp.zeros((total, na * rank), F32)
+    turned = jnp.zeros((na * rank, total), F32)
     for k in range(kvl):
         for d in range(1, n):
             o = peer_z(d)
             rcopy(att.at[k, o], att.at[k, o], att_ss.at[k, o], att_rs.at[k, o], "adapter", o).wait_recv()
         every = att[k].reshape(total, half)
-        racc = racc + mm(every, odc[k * half:(k + 1) * half])
+        turned = turned + mm(odown_v[:, k * half:(k + 1) * half], every, ((1,), (1,)))
         if k == kvl - 1:
-            turned = racc.T
             turned = jnp.where(ad_row == z * na + iota((na * rank, total), 0) // rank, turned, 0.0)
             ranks = turned[:rank]
             for a in range(1, na):
@@ -261,39 +288,35 @@
             rl = rank // nh
             for p in range(nh):
                 rr_out[p] = ranks[p * rl:(p + 1) * rl]
-            for d in range(1, nh):
-                p = peer_h(d)
-                cp = rcopy(rr_out.at[p], rr_in.at[h], rr_ss.at[p], rr_rs.at[h], "head", p)
-                cp.start()
-                sends.append(cp)
+            rr_in[me] = rr_out[h]
+
+            @pl.loop(1, plane)
+            def _(d):
+                other, dev = plane_dev(d)
+                rcopy(rr_out.at[lax.rem(other, nh)], rr_in.at[me],
+                      rr_ss.at[other], rr_rs.at[me], None, dev).start()
+
         for c in range(nc):
             term = mm(every, w_v[k * half:(k + 1) * half, c * cw:(c + 1) * cw])
             if k == 0:
                 tot[c] = term
             else:
                 tot[c] = tot[c] + term
-            if k == kvl - 1 and c == 0:
-                summed = rr_out[h]
-                for d in range(1, nh):
-                    p = peer_h(d)
-                    rcopy(rr_out.at[p], rr_in.at[p], rr_ss.at[p], rr_rs.at[p], "head", p).wait_recv()
-                    summed = summed + rr_in[p]
-                ag[z] = summed
-                for d in range(1, n):
-                    o = peer_z(d)
-                    cp = rcopy(ag.at[z], ag.at[z], ag_ss.at[o], ag_rs.at[z], "adapter", o)
-                    cp.start()
-                    sends.append(cp)
 
     for d in range(1, n):
         o = peer_z(d)
-        rcopy(ag.at[o], ag.at[o], ag_ss.at[o], ag_rs.at[o], "adapter", o).wait_recv()
-        rcopy(oup_hbm.at[:, pl.ds(pl.multiple_of(o * cols, 128), cols)], up_all.at[o],
-              up_ss.at[o], up_rs.at[o], "adapter", o).wait_recv()
+        for e in range(1, ng):
+            y = lax.rem(gi + e, ng)
+            rcopy(up_part(o, y), up_part(o, y), y_ss.at[y, o], y_rs.at[y, o], "groups", y).wait_recv()
+
+    @pl.loop(1, plane)
+    def _(d):
+        other, dev = plane_dev(d)
+        rcopy(rr_out.at[lax.rem(other, nh)], rr_in.at[other],
+              rr_ss.at[other], rr_rs.at[other], None, dev).wait()
+
     own_up.wait()
-    mine_ranks = ag[0]
-    for o in range(1, n):
-        mine_ranks = mine_ranks + ag[o]
+    mine_ranks = jnp.sum(rr_in[...], axis=0)
     rl = rank // nh
     kk = n * na * rl
     tile = (lax.rem(iota((rl, kk), 1), rl) == iota((rl, kk), 0)).astype(F32).astype(BF)
@@ -339,6 +362,7 @@
 ):
     n = lax.axis_size("adapter")
     nh = lax.axis_size("head")
+    ng = lax.axis_size("groups")
     rows, feats = normed_hidden_rows.shape
     total = planned_request_rows.shape[0]
     na, _, rank = output_down_maps.shape
@@ -348,7 +372,7 @@
     kvw = base_key_value.shape[2]
     kvl = kvw // HD
     half = qw // kvl
-    dw = qw + 2 * kvw
+    dw = half + 2 * HD
     cols = output_weight_matrix.shape[1]
     cw = min(512, cols)
     nc = cols // cw
@@ -361,6 +385,8 @@
     hb = pl.BlockSpec(memory_space=pl.ANY)
     dma = pltpu.SemaphoreType.DMA
     ups = output_up_maps.reshape(na * output_up_maps.shape[1], -1)
+    downs = jnp.swapaxes(query_key_value_down_maps, 1, 2).reshape(na * 3 * rank, feats)
+    odowns = jnp.swapaxes(output_down_maps, 1, 2).reshape(na * rank, qw)
     qups = query_up_maps.reshape(na * rank, qw)
     return pl.pallas_call(
         functools.partial(kernel, (n, nh, rows, slot, na, rank)),
@@ -369,36 +395,34 @@
         out_specs=vm,
         scratch_shapes=[
             pltpu.VMEM(key_value_cache.shape, BF),
-            pltpu.VMEM(query_key_value_down_maps.shape, BF),
+            pltpu.VMEM(downs.shape, BF),
             pltpu.VMEM(qups.shape, BF),
             pltpu.VMEM(key_value_up_maps.shape, BF),
-            pltpu.VMEM(output_down_maps.shape, BF),
+            pltpu.VMEM(odowns.shape, BF),
             pltpu.VMEM(output_weight_matrix.shape, BF),
             pltpu.VMEM((n, slot, feats), BF),
             pltpu.VMEM((n, slot, feats), BF),
             pltpu.VMEM((cells, 3 * rank), F32),
             pltpu.VMEM((nh, cells, 3 * rank), F32),
-            pltpu.VMEM((n, slot, dw), BF),
-            pltpu.VMEM((n, slot, dw), BF),
+            pltpu.VMEM((kvl, n, slot, dw), BF),
+            pltpu.VMEM((kvl, n, slot, dw), BF),
             pltpu.VMEM((n, ups.shape[0], cols), BF),
-            pltpu.VMEM((output_down_maps.shape[1], na * rank), BF),
             pltpu.VMEM((pages // CHUNK_PAGES, rows, ct), F32),
             pltpu.VMEM((pages // CHUNK_PAGES, gr, ct), F32),
             pltpu.VMEM((kvl, n, rows, half), BF),
             pltpu.VMEM((nc, total, cw), F32),
             pltpu.VMEM((nh, rl, total), F32),
-            pltpu.VMEM((nh, rl, total), F32),
-            pltpu.VMEM((n, rl, total), F32),
+            pltpu.VMEM((n * nh, rl, total), F32),
             pltpu.VMEM((nc, nh, out_rows, cw), BF),
             pltpu.VMEM((nc, nh, out_rows, cw), BF),
             dma((7,)),
             dma((n,)), dma((n,)),
             dma((nh,)), dma((nh,)),
+            dma((kvl, n)), dma((kvl, n)),
             dma((n,)), dma((n,)),
-            dma((n,)), dma((n,)),
+            dma((ng, n)), dma((ng, n)),
             dma((kvl, n)), dma((kvl, n)),
-            dma((nh,)), dma((nh,)),
-            dma((n,)), dma((n,)),
+            dma((n * nh,)), dma((n * nh,)),
             dma((nc, nh)), dma((nc, nh)),
         ],
         compiler_params=pltpu.CompilerParams(
@@ -407,8 +431,8 @@
         normed_hidden_rows, base_query, base_key_value,
         cached_length_per_request.reshape(1, rows), request_page_table,
         planned_request_rows.reshape(1, total), request_adapters.reshape(1, total),
-        key_value_cache, query_key_value_down_maps, qups, key_value_up_maps,
-        output_down_maps, ups, output_weight_matrix,
+        key_value_cache, downs, qups, key_value_up_maps,
+        odowns, ups, output_weight_matrix,
     )
 
 

time: 71.4 us -> 59 us (0.83)
  Pallas kernels: 64.1 us -> 57.3 us
  local copies, waits for them, and re-layouts: 7.1 us -> 1.57 us
    pallas_call x1, Pallas kernels: 64.1 us -> 57.3 us  [body(): pl.pallas_call(functools.partial(kernel, (n, nh, rows, slot, na, rank)),...]
    unnamed x5 -> x1, local copies, waits for them, and re-layouts: 7.1 us -> 1.57 us
where the time goes in v2:
time: 59 us; the launch traced here: 58.8 us
  Pallas kernels  57.3 us (97%)
  local copies, waits for them, and re-layouts  1.57 us (3%)
    pallas_call x1, Pallas kernels, body(): pl.pallas_call(functools.partial(kernel, (n, nh, rows, slot, na, rank)),...  57.3 us
    unnamed x1, local copies, waits for them, and re-layouts  1.57 us

profile of v2, /device:TPU:0, one launch (start us, length us, event | category | flops | bytes accessed | tf_op | source)
XLA Modules:
  0.0 58.8 jit_solution(18352513376445987272)
XLA Ops:
  0.0 57.3 %shard_map.136 = bf16[32,2048]{1,0:T(8,128)(2,1)} custom-call(bf16[32,2048]{1,0:T(8,128)(2,1)} %hid_ref.1, bf16[32,2048]{1,0:T(8,128)(2,1)} %bq_ref.1, bf16[32,2,256]{2,1,0:T(2,128)(2,1)} %bkv_ref.1, s32[1,32]{1,0:T(1,128)} %bitcast.15, s32[32,160]{1,0:T(8,128)} %table_ref.1, s32[1,128]{1,0:T(1,128)} %bitcast.16, s32[1,128]{1,0:T(1,128)} %bitcast.17, ...), custom_call_target="tpu_custom_call" | custom-call | tf_op jit(solution)/shard_map/pallas_call | solution.py:391
  57.3 1.6 %copy.16 = bf16[32,2048]{1,0:T(8,128)(2,1)} copy(bf16[32,2048]{1,0:T(8,128)(2,1)} %shard_map.136) | data formatting | bytes 262144

commit v3 on v2

--- a/solution.py
+++ b/solution.py
@@ -32,9 +32,9 @@
     out_ref,
     cache_v, down_v, qup_v, kvup_v, odown_v, w_v,
     row_out, row_in, ps_out, ps_in, dl_out, dl_in, up_all,
-    bias_s, score_s, att, tot, rr_out, rr_in, fin_out, fin_in,
+    bias_s, score_s, att, tot, rr_out, rr_in, sa_out, sa_in, fin_out, fin_in,
     lsem, row_ss, row_rs, ps_ss, ps_rs, dl_ss, dl_rs, up_ss, up_rs,
-    y_ss, y_rs, att_ss, att_rs, rr_ss, rr_rs, fin_ss, fin_rs,
+    y_ss, y_rs, att_ss, att_rs, rr_ss, rr_rs, sa_ss, sa_rs, fin_ss, fin_rs,
 ):
     n, nh, rows, slot, na, rank = cfg
     total = n * rows
@@ -221,6 +221,30 @@
             sends.append(cp)
     locals_[3].wait()
 
+    def hop(k, o, way):
+        to = lax.rem(z + 1, n) if way == 0 else lax.rem(z + n - 1, n)
+        return rcopy(att.at[k, o], att.at[k, o], att_ss.at[way, k, o], att_rs.at[k, o], "adapter", to)
+
+    def arrive(k, d):
+        low = jnp.maximum(z - d, 0)
+        high = jnp.minimum(z + d, n - 1)
+
+        @pl.when(z >= d)
+        def _():
+            hop(k, low, 0).wait_recv()
+
+        @pl.when((z >= d) & (z < n - 1))
+        def _():
+            hop(k, low, 0).start()
+
+        @pl.when(z + d < n)
+        def _():
+            hop(k, high, 1).wait_recv()
+
+        @pl.when((z + d < n) & (z > 0))
+        def _():
+            hop(k, high, 1).start()
+
     scale = HD ** -0.5 * math.log2(math.e)
     gr = group * rows
     for k in range(kvl):
@@ -264,20 +288,19 @@
         mixed = ((acc + own_w * vn) / den).astype(BF)
         for g in range(group):
             att[k, z, :, g * HD:(g + 1) * HD] = mixed[g * rows:(g + 1) * rows]
-        for d in range(1, n):
-            o = peer_z(d)
-            cp = rcopy(att.at[k, z], att.at[k, z], att_ss.at[k, o], att_rs.at[k, z], "adapter", o)
-            cp.start()
-            sends.append(cp)
+        pl.when(z < n - 1)(lambda k=k: hop(k, z, 0).start())
+        pl.when(z > 0)(lambda k=k: hop(k, z, 1).start())
 
     locals_[4].wait()
     locals_[5].wait()
     nc, _, cw = tot.shape
     turned = jnp.zeros((na * rank, total), F32)
+    for d in range(1, n):
+        for k in range(kvl if d < n - 1 else 1):
+            arrive(k, d)
     for k in range(kvl):
-        for d in range(1, n):
-            o = peer_z(d)
-            rcopy(att.at[k, o], att.at[k, o], att_ss.at[k, o], att_rs.at[k, o], "adapter", o).wait_recv()
+        if k > 0:
+            arrive(k, n - 1)
         every = att[k].reshape(total, half)
         turned = turned + mm(odown_v[:, k * half:(k + 1) * half], every, ((1,), (1,)))
         if k == kvl - 1:
@@ -323,23 +346,48 @@
     sel = mm(mine_ranks.astype(BF), tile, ((0,), (0,)))
     sel = jnp.where(ad_col == iota((total, kk), 1) // rl, sel * 0.5, 0.0).astype(BF)
     out_rows = total // nh
+    nx = nh // 2
+    xi = h // 2
+    core = lax.rem(h, 2)
+    sibling = 2 * xi + 1 - core
+
+    def block(c, p):
+        return tot[c, pl.ds(pl.multiple_of(p * out_rows, 8), out_rows), :]
+
     for c in range(nc):
         ups = up_all[:, :, c * cw:(c + 1) * cw].reshape(kk, cw)
         full = tot[c] + mm(sel, ups)
         tot[c] = full
-        fin_out[c] = full.astype(BF).reshape(nh, out_rows, cw)
-        for d in range(1, nh):
-            p = peer_h(d)
-            cp = rcopy(fin_out.at[c, p], fin_in.at[c, h], fin_ss.at[c, p], fin_rs.at[c, h], "head", p)
+        for x in range(nx):
+            sa_out[c, x] = block(c, 2 * x + 1 - core).astype(BF)
+        cp = rcopy(sa_out.at[c], sa_in.at[c], sa_ss.at[c], sa_rs.at[c], "head", sibling)
+        cp.start()
+        sends.append(cp)
+    for c in range(nc):
+        rcopy(sa_out.at[c], sa_in.at[c], sa_ss.at[c], sa_rs.at[c], "head", sibling).wait_recv()
+        for d in range(1, nx):
+            x = lax.rem(xi + d, nx)
+            fin_out[c, x] = (block(c, 2 * x + core) + sa_in[c, x].astype(F32)).astype(BF)
+            cp = rcopy(fin_out.at[c, x], fin_in.at[c, xi], fin_ss.at[c, x], fin_rs.at[c, xi],
+                       "head", 2 * x + core)
             cp.start()
             sends.append(cp)
     for c in range(nc):
-        res = tot[c, pl.ds(pl.multiple_of(h * out_rows, 8), out_rows), :]
-        for d in range(1, nh):
-            p = peer_h(d)
-            rcopy(fin_out.at[c, p], fin_in.at[c, p], fin_ss.at[c, p], fin_rs.at[c, p], "head", p).wait_recv()
-            res = res + fin_in[c, p].astype(F32)
+        res = block(c, h) + sa_in[c, xi].astype(F32)
+        for d in range(1, nx):
+            x = lax.rem(xi + d, nx)
+            rcopy(fin_out.at[c, x], fin_in.at[c, x], fin_ss.at[c, x], fin_rs.at[c, x],
+                  "head", 2 * x + core).wait_recv()
+            res = res + fin_in[c, x].astype(F32)
         out_ref[:, c * cw:(c + 1) * cw] = res.astype(BF)
+    for k in range(kvl):
+        pl.when(z < n - 1)(lambda k=k: hop(k, z, 0).wait_send())
+        pl.when(z > 0)(lambda k=k: hop(k, z, 1).wait_send())
+        for d in range(1, n):
+            pl.when((z >= d) & (z < n - 1))(
+                lambda k=k, d=d: hop(k, jnp.maximum(z - d, 0), 0).wait_send())
+            pl.when((z + d < n) & (z > 0))(
+                lambda k=k, d=d: hop(k, jnp.minimum(z + d, n - 1), 1).wait_send())
     for cp in sends:
         cp.wait_send()
 
@@ -413,17 +461,20 @@
             pltpu.VMEM((nc, total, cw), F32),
             pltpu.VMEM((nh, rl, total), F32),
             pltpu.VMEM((n * nh, rl, total), F32),
-            pltpu.VMEM((nc, nh, out_rows, cw), BF),
-            pltpu.VMEM((nc, nh, out_rows, cw), BF),
+            pltpu.VMEM((nc, nh // 2, out_rows, cw), BF),
+            pltpu.VMEM((nc, nh // 2, out_rows, cw), BF),
+            pltpu.VMEM((nc, nh // 2, out_rows, cw), BF),
+            pltpu.VMEM((nc, nh // 2, out_rows, cw), BF),
             dma((7,)),
             dma((n,)), dma((n,)),
             dma((nh,)), dma((nh,)),
             dma((kvl, n)), dma((kvl, n)),
             dma((n,)), dma((n,)),
             dma((ng, n)), dma((ng, n)),
-            dma((kvl, n)), dma((kvl, n)),
+            dma((2, kvl, n)), dma((kvl, n)),
             dma((n * nh,)), dma((n * nh,)),
-            dma((nc, nh)), dma((nc, nh)),
+            dma((nc,)), dma((nc,)),
+            dma((nc, nh // 2)), dma((nc, nh // 2)),
         ],
         compiler_params=pltpu.CompilerParams(
             collective_id=0, has_side_effects=True, vmem_limit_bytes=58 * 1024 * 1024),

time: 59 us -> 58.7 us (level)
  no operation moved by 1% of the time
where the time goes in v3:
time: 58.7 us; the launch traced here: 58.6 us
  Pallas kernels  57 us (97%)
  local copies, waits for them, and re-layouts  1.57 us (3%)
    pallas_call x1, Pallas kernels, body(): pl.pallas_call(functools.partial(kernel, (n, nh, rows, slot, na, rank)),...  57 us
    unnamed x1, local copies, waits for them, and re-layouts  1.57 us

profile of v3, /device:TPU:0, one launch (start us, length us, event | category | flops | bytes accessed | tf_op | source)
XLA Modules:
  0.0 58.6 jit_solution(6793112013752422988)
XLA Ops:
  0.0 57.0 %shard_map.136 = bf16[32,2048]{1,0:T(8,128)(2,1)} custom-call(bf16[32,2048]{1,0:T(8,128)(2,1)} %hid_ref.1, bf16[32,2048]{1,0:T(8,128)(2,1)} %bq_ref.1, bf16[32,2,256]{2,1,0:T(2,128)(2,1)} %bkv_ref.1, s32[1,32]{1,0:T(1,128)} %bitcast.15, s32[32,160]{1,0:T(8,128)} %table_ref.1, s32[1,128]{1,0:T(1,128)} %bitcast.16, s32[1,128]{1,0:T(1,128)} %bitcast.17, ...), custom_call_target="tpu_custom_call" | custom-call | tf_op jit(solution)/shard_map/pallas_call | solution.py:439
  57.0 1.6 %copy.16 = bf16[32,2048]{1,0:T(8,128)(2,1)} copy(bf16[32,2048]{1,0:T(8,128)(2,1)} %shard_map.136) | data formatting | bytes 262144

commit v4 on v3

--- a/solution.py
+++ b/solution.py
@@ -68,12 +68,12 @@
         (cache_hbm, cache_v), (odown_hbm, odown_v), (w_hbm, w_v),
     )):
         cp = pltpu.make_async_copy(src, dst, lsem.at[i])
-        cp.start()
+        if i < 3:
+            cp.start()
         locals_.append(cp)
     own_up = pltpu.make_async_copy(
         oup_hbm.at[:, pl.ds(pl.multiple_of(z * w_v.shape[1], 128), w_v.shape[1])],
         up_all.at[z], lsem.at[6])
-    own_up.start()
 
     barrier = pltpu.get_barrier_semaphore()
 
@@ -128,6 +128,10 @@
         cp = rcopy(row_out.at[o], row_in.at[z], row_ss.at[o], row_rs.at[z], "adapter", o)
         cp.start()
         sends.append(cp)
+
+    for cp in locals_[3:]:
+        cp.start()
+    own_up.start()
 
     pages = cache_v.shape[0]
     page_len = cache_v.shape[2]

time: 58.7 us -> 58.6 us (level)
  no operation moved by 1% of the time
where the time goes in v4:
time: 58.6 us; the launch traced here: 58.5 us
  Pallas kernels  56.9 us (97%)
  local copies, waits for them, and re-layouts  1.57 us (3%)
    pallas_call x1, Pallas kernels, body(): pl.pallas_call(functools.partial(kernel, (n, nh, rows, slot, na, rank)),...  56.9 us
    unnamed x1, local copies, waits for them, and re-layouts  1.57 us

profile of v4, /device:TPU:0, one launch (start us, length us, event | category | flops | bytes accessed | tf_op | source)
XLA Modules:
  0.0 58.5 jit_solution(2859379014943703588)
XLA Ops:
  0.0 56.9 %shard_map.136 = bf16[32,2048]{1,0:T(8,128)(2,1)} custom-call(bf16[32,2048]{1,0:T(8,128)(2,1)} %hid_ref.1, bf16[32,2048]{1,0:T(8,128)(2,1)} %bq_ref.1, bf16[32,2,256]{2,1,0:T(2,128)(2,1)} %bkv_ref.1, s32[1,32]{1,0:T(1,128)} %bitcast.15, s32[32,160]{1,0:T(8,128)} %table_ref.1, s32[1,128]{1,0:T(1,128)} %bitcast.16, s32[1,128]{1,0:T(1,128)} %bitcast.17, ...), custom_call_target="tpu_custom_call" | custom-call | tf_op jit(solution)/shard_map/pallas_call | solution.py:443
  56.9 1.6 %copy.16 = bf16[32,2048]{1,0:T(8,128)(2,1)} copy(bf16[32,2048]{1,0:T(8,128)(2,1)} %shard_map.136) | data formatting | bytes 262144
